TPU v7x, 768 devices: a whole 4x8x12 slice. The times are simulated.
768 devices in a mesh: replica: 32 (over y, x), expert: 24 (over z, core).
Axes of the slice: x: 4, y: 8, z: 12, core: 2. Of those that a mesh axis runs over, the one named last changes fastest.
Arguments:
- tokens: bfloat16 [32, 3072, 1024], P('replica', 'expert'), may hold values from -6 to 6
- cotangent: bfloat16 [32, 3072, 1024], P('replica', 'expert'), may hold values from -6 to 6
- w_in: bfloat16 [24, 1024, 2048], P('expert'), may hold values from -0.1875 to 0.1875
- w_out: bfloat16 [24, 2048, 1024], P('expert'), may hold values from -0.125 to 0.125
- gate_values: float32 [32, 24, 192], P('replica', 'expert'), may hold values from 0.05 to 1
- expert_ids: int32 [32, 24, 192], P('replica', 'expert'), may hold values from 0 to 3071, as said below
- valid_counts: int32 [32, 24], P('replica', 'expert'), may hold values from 10 to 192
Outputs:
- mixed_rows: bfloat16 [32, 3072, 1024], P('replica', 'expert')
- token_grad: bfloat16 [32, 3072, 1024], P('replica', 'expert')
- grad_w_in: bfloat16 [24, 1024, 2048], P('expert', 'replica')
- grad_w_out: bfloat16 [24, 2048, 1024], P('expert', 'replica')
Inputs may be any that keep to these rules, and one draw needn't show every extreme that they name: `expert_ids`: live entries of an expert's list are distinct and ascending; entries past the live count are 0. Among the live entries of one list, at most 10 lie in one device's block of 128 tokens, and some list has exactly 10 in some block.
All inputs are finite; a program needn't handle non-finite values.
Results may differ from a plain program's by a relative error of at most 0.02.
Values may be sent and summed in bfloat16 or wider, within the bound.
A program may use at most 64 MiB of HBM per device.

v0:
```python
import jax
import jax.numpy as jnp
from jax import lax
from jax.sharding import PartitionSpec as P

MOST = 10


def gelu_value(values):
    return 0.5 * values * (1.0 + jax.scipy.special.erf(values * 0.7071067811865476))


def gelu_slope(values):
    return (
        0.5 * (1.0 + jax.scipy.special.erf(values * 0.7071067811865476))
        + values * jnp.exp(-0.5 * values * values) * 0.3989422804014327
    )


def contract_rows(left, right):
    return lax.dot_general(
        left, right, (((0,), (0,)), ((), ())), preferred_element_type=jnp.bfloat16
    )


def contract_cols(left, right):
    return lax.dot_general(
        left, right, (((1,), (1,)), ((), ())), preferred_element_type=jnp.float32
    )


def per_device(tokens, cotangent, w_in, w_out, gate_values, expert_ids, valid_counts):
    own_tokens = tokens[0]
    own_cot = cotangent[0]
    tok_rows = own_tokens.shape[0]
    feature_count = own_tokens.shape[1]
    capacity = expert_ids.shape[2]
    expert_count = lax.axis_size("expert")
    myself = lax.axis_index("expert")
    zero_bf = jnp.zeros((), jnp.bfloat16)
    all_ids, all_counts = (
        lax.all_gather(expert_ids[0], "expert", axis=0, tiled=True),
        lax.all_gather(valid_counts[0], "expert", axis=0, tiled=True),
    )
    slot_index = jnp.arange(capacity, dtype=jnp.int32)
    valid_all = slot_index[None, :] < all_counts[:, None]
    source_all = all_ids // tok_rows
    source_index = jnp.arange(expert_count, dtype=jnp.int32)
    starts = jnp.sum(
        (valid_all[:, :, None] & (source_all[:, :, None] < source_index)).astype(jnp.int32), axis=1
    )
    pair_sizes = jnp.sum(
        (valid_all[:, :, None] & (source_all[:, :, None] == source_index)).astype(jnp.int32), axis=1
    )
    depth_index = jnp.arange(MOST, dtype=jnp.int32)
    send_start = starts[:, myself]
    send_size = pair_sizes[:, myself]
    send_ok = depth_index[None, :] < send_size[:, None]
    send_slot = jnp.minimum(send_start[:, None] + depth_index[None, :], capacity - 1)
    send_local = jnp.where(
        send_ok, jnp.take_along_axis(all_ids, send_slot, axis=1) - myself * tok_rows, 0
    )
    own_ids = expert_ids[0, 0]
    own_valid = slot_index < valid_counts[0, 0]
    own_starts = starts[myself]
    own_sizes = pair_sizes[myself]
    outgoing = jnp.where(send_ok[:, :, None], own_tokens[send_local], zero_bf)
    outgoing_cot = jnp.where(send_ok[:, :, None], own_cot[send_local], zero_bf)
    arrived, arrived_cot = (
        lax.all_to_all(outgoing, "expert", split_axis=0, concat_axis=0, tiled=True),
        lax.all_to_all(outgoing_cot, "expert", split_axis=0, concat_axis=0, tiled=True),
    )
    own_source = jnp.clip(own_ids // tok_rows, 0, expert_count - 1)
    flat_slot = jnp.where(own_valid, own_source * MOST + slot_index - own_starts[own_source], 0)
    picked = jnp.where(own_valid[:, None], arrived.reshape(-1, feature_count)[flat_slot], zero_bf)
    picked_cot = jnp.where(
        own_valid[:, None], arrived_cot.reshape(-1, feature_count)[flat_slot], zero_bf
    )
    gate_row = gate_values[0, 0]
    in_weight = w_in[0]
    out_weight = w_out[0]
    before = jnp.dot(picked, in_weight, preferred_element_type=jnp.float32)
    hidden = gelu_value(before).astype(jnp.bfloat16)
    projected = jnp.dot(hidden, out_weight, preferred_element_type=jnp.float32)
    weighted = (gate_row[:, None] * projected).astype(jnp.bfloat16)
    upstream = (gate_row[:, None] * picked_cot.astype(jnp.float32)).astype(jnp.bfloat16)
    term_out = contract_rows(hidden, upstream)
    hidden_grad = contract_cols(upstream, out_weight)
    before_grad = (hidden_grad * gelu_slope(before)).astype(jnp.bfloat16)
    input_grad = contract_cols(before_grad, in_weight).astype(jnp.bfloat16)
    term_in = contract_rows(picked, before_grad)
    sum_in, sum_out = (
        lax.psum_scatter(term_in[None], "replica", scatter_dimension=1, tiled=True).astype(
            jnp.float32
        ),
        lax.psum_scatter(term_out[None], "replica", scatter_dimension=1, tiled=True).astype(
            jnp.float32
        ),
    )
    back_ok = depth_index[None, :] < own_sizes[:, None]
    back_slot = jnp.minimum(own_starts[:, None] + depth_index[None, :], capacity - 1)
    back_rows = jnp.where(back_ok[:, :, None], weighted[back_slot], zero_bf)
    back_grad = jnp.where(back_ok[:, :, None], input_grad[back_slot], zero_bf)
    returned, returned_grad = (
        lax.all_to_all(back_rows, "expert", split_axis=0, concat_axis=0, tiled=True),
        lax.all_to_all(back_grad, "expert", split_axis=0, concat_axis=0, tiled=True),
    )
    token_index = jnp.arange(tok_rows, dtype=jnp.int32)
    selector = (
        (send_local.reshape(-1)[None, :] == token_index[:, None]) & send_ok.reshape(-1)[None, :]
    ).astype(jnp.bfloat16)
    mixed_rows = jnp.dot(
        selector, returned.reshape(-1, feature_count), preferred_element_type=jnp.float32
    ).astype(jnp.bfloat16)
    token_grad = jnp.dot(
        selector, returned_grad.reshape(-1, feature_count), preferred_element_type=jnp.float32
    ).astype(jnp.bfloat16)
    replicas = lax.axis_size("replica")
    grad_w_in = (sum_in / replicas).astype(jnp.bfloat16)
    grad_w_out = (sum_out / replicas).astype(jnp.bfloat16)
    return (mixed_rows[None], token_grad[None], grad_w_in, grad_w_out)


def solution(mesh):
    placed = (
        P("replica", "expert", None),
        P("replica", "expert", None),
        P("expert", None, None),
        P("expert", None, None),
        P("replica", "expert", None),
        P("replica", "expert", None),
        P("replica", "expert"),
    )
    return jax.shard_map(
        per_device,
        mesh=mesh,
        in_specs=placed,
        out_specs=(
            P("replica", "expert", None),
            P("replica", "expert", None),
            P("expert", "replica", None),
            P("expert", "replica", None),
        ),
        check_vma=False,
    )
```

profile of v0, /device:TPU:16, one launch (start us, length us, event | category | flops | bytes accessed | tf_op | source)
XLA Modules:
  0.0 640.4 jit_solution(2910545448496126292)
XLA Ops:
  7.2 33.5 %all-gather.1 = s32[24,1,192]{2,1,0:T(1,128)S(1)} all-gather(s32[1,1,192]{2,1,0:T(1,128)} %param.12), channel_id=3, replica_groups=mesh['replica'=32,'expert'=24] {'expert'}, dimensions={0}, use_global_device_ids=true | all-gather | bytes 19200 | tf_op jit(solution)/shard_map/all_gather | solution.py:42
  41.4 1.3 dynamic-slice
  43.4 35.0 %all-reduce = s32[24]{0:T(128)S(1)} all-reduce(s32[24]{0:T(128)S(1)} %bitcast_dynamic-update-slice_fusion), channel_id=2, replica_groups=mesh['replica'=32,'expert'=24] {'expert'}, use_global_device_ids=true, to_apply=%add | all-reduce | flops 24 | bytes 192
  79.7 3.6 gather_fusion.6
  83.6 1.1 gather_fusion
  85.7 1.1 gather_fusion.3
  87.0 1.1 broadcast_select_fusion
  88.1 36.2 %all_to_all.20 = bf16[24,10,1024]{2,1,0:T(8,128)(2,1)S(1)} all-to-all(bf16[24,10,1024]{2,1,0:T(8,128)(2,1)S(1)} %get-tuple-element.28), channel_id=1, replica_groups=mesh['replica'=32,'expert'=24] {'expert'}, dimensions={0} | all-to-all | bytes 983040 | tf_op jit(solution)/shard_map/all_to_all | solution.py:71
  124.3 3.9 all-to-all-start
  129.7 4.4 compare_select_fusion.5
  134.2 10.6 %select_select_fusion = s32[192]{0:T(256)S(1)} fusion(pred[192]{0:T(512)(128)(4,1)S(1)} %get-tuple-element.22, pred[192]{0:T(512)(128)(4,1)S(1)} %get-tuple-element.21, pred[192]{0:T(512)(128)(4,1)S(1)} %get-tuple-element.20, pred[192]{0:T(512)(128)(4,1)S(1)} %get-tuple-element.19, pred[192]{0:T(512)(128)(4,1)S(1)} %get-tuple-element.18, ...), kind=kLoop, calls=%fused_computation.112 | loop fusion | flops 3264 | bytes 4868 | tf_op jit(solution)/shard_map/gather | solution.py:74
  145.0 1.0 gather_fusion.4
  146.0 15.3 %all-to-all-done = bf16[24,10,1024]{2,1,0:T(8,128)(2,1)S(1)} async-done(((bf16[24,10,1024]{2,1,0:T(8,128)(2,1)}), bf16[24,10,1024]{2,1,0:T(8,128)(2,1)S(1)}, u32[]{:S(2)}, u32[]{:S(2)}) %all-to-all-start) | async-done | bytes 491552 | tf_op jit(solution)/shard_map/all_to_all | solution.py:70
  161.5 1.0 gather_fusion.1
  162.5 3.2 fusion.6
  165.7 3.4 convolution_bitcast_fusion
  169.3 4.0 fusion.11
  174.3 3.4 convolution_bitcast_fusion.1
  178.8 3.7 fusion.24
  182.5 1.1 gather_fusion.5
  183.8 3.2 fusion.21
  187.1 1.1 gather_fusion.2
  188.4 1.1 broadcast_select_fusion.2
  189.5 36.5 %all_to_all.21 = bf16[24,10,1024]{2,1,0:T(8,128)(2,1)S(1)} all-to-all(bf16[24,10,1024]{2,1,0:T(8,128)(2,1)S(1)} %get-tuple-element.26), channel_id=1, replica_groups=mesh['replica'=32,'expert'=24] {'expert'}, dimensions={0} | all-to-all | bytes 983040 | tf_op jit(solution)/shard_map/all_to_all | solution.py:106
  225.9 3.9 all-to-all-start.1
  230.4 32.5 %all-to-all-done.1 = bf16[24,10,1024]{2,1,0:T(8,128)(2,1)S(1)} async-done(((bf16[24,10,1024]{2,1,0:T(8,128)(2,1)}), bf16[24,10,1024]{2,1,0:T(8,128)(2,1)S(1)}, u32[]{:S(2)}, u32[]{:S(2)}) %all-to-all-start.1) | async-done | bytes 491552 | tf_op jit(solution)/shard_map/all_to_all | solution.py:105
  263.1 0.9 fusion.28
  264.0 0.9 fusion.27
  264.9 130.5 %reduce-scatter.5.cloned.1.call-done = bf16[1,64,1024]{2,1,0:T(8,128)(2,1)} async-done(((bf16[1,2048,1024]{2,1,0:T(8,128)(2,1)}), bf16[1,64,1024]{2,1,0:T(8,128)(2,1)}) %reduce-scatter.5.cloned.1.call-update) | async-done | bytes 131088 | tf_op jit(solution)/shard_map/reduce_scatter | solution.py:96
  395.4 1.6 multiply_convert_fusion.2
  397.0 235.0 %reduce-scatter.3.cloned.1.call-done = bf16[1,32,2048]{2,1,0:T(8,128)(2,1)} async-done(((bf16[1,1024,2048]{2,1,0:T(8,128)(2,1)}), bf16[1,32,2048]{2,1,0:T(8,128)(2,1)}) %reduce-scatter.3.cloned.1.call-update) | async-done | bytes 131088 | tf_op jit(solution)/shard_map/reduce_scatter | solution.py:93
  632.0 1.6 multiply_convert_fusion.3
  (57 shorter events, 8.7 us)
Async XLA Ops:
  7.2 76.5 %copy-start = (bf16[1,128,1024]{2,1,0:T(8,128)(2,1)S(1)}, bf16[1,128,1024]{2,1,0:T(8,128)(2,1)}, u32[]{:S(2)}) copy-start(bf16[1,128,1024]{2,1,0:T(8,128)(2,1)} %param.7) | copy-start | bytes 786436
  84.8 1.0 copy-start.1
  88.1 41.6 %copy-start.2 = (s32[1,1,192]{2,1,0:T(1,128)S(1)}, s32[1,1,192]{2,1,0:T(1,128)}, u32[]{:S(2)}) copy-start(s32[1,1,192]{2,1,0:T(1,128)} %param.12) | copy-start | bytes 2308
  124.3 36.9 %all-to-all-start = ((bf16[24,10,1024]{2,1,0:T(8,128)(2,1)}), bf16[24,10,1024]{2,1,0:T(8,128)(2,1)S(1)}, u32[]{:S(2)}, u32[]{:S(2)}) async-start(bf16[24,10,1024]{2,1,0:T(8,128)(2,1)} %get-tuple-element.29), calls=%async_computation | async-start | bytes 1572864 | tf_op jit(solution)/shard_map/all_to_all | solution.py:70
  128.2 267.2 %reduce-scatter.5.cloned.1.call-start = ((), (), s32[]{:S(2)}) async-start(), calls=%async_computation.7 | async-start | bytes 4325376 | tf_op jit(solution)/shard_map/reduce_scatter | solution.py:96
  162.5 3.2 copy-start.3
  169.1 462.9 %reduce-scatter.3.cloned.1.call-start = ((), (), s32[]{:S(2)}) async-start(), calls=%async_computation.6 | async-start | bytes 4325376 | tf_op jit(solution)/shard_map/reduce_scatter | solution.py:93
  173.4 0.9 copy-start.4
  177.7 1.1 copy-start.5
  225.9 36.9 %all-to-all-start.1 = ((bf16[24,10,1024]{2,1,0:T(8,128)(2,1)}), bf16[24,10,1024]{2,1,0:T(8,128)(2,1)S(1)}, u32[]{:S(2)}, u32[]{:S(2)}) async-start(bf16[24,10,1024]{2,1,0:T(8,128)(2,1)} %get-tuple-element.27), calls=%async_computation.1 | async-start | bytes 1572864 | tf_op jit(solution)/shard_map/all_to_all | solution.py:105
Sparse Core Ops, SparseCore 0:
  169.2 226.1 reduce-scatter.4
  401.3 230.6 reduce-scatter.2
where the time goes:
time: 641 us; the launch traced here: 640 us
  waiting for transfers between devices  413 us (64%)
  blocking collectives  141 us (22%)
  matrix products  22.8 us (4%)
  other arithmetic  21.8 us (3%)
  local copies, waits for them, and re-layouts  18.3 us (3%)
  between operations  15 us (2%)
  starting transfers between devices  8.05 us (1%)
    reduce_scatter x1, waiting for transfers between devices, per_device(): lax.psum_scatter(term_in[None], 'replica', scatter_dimension=1, tiled=True)  235 us
    reduce_scatter x1, waiting for transfers between devices, per_device(): lax.psum_scatter(term_out[None], 'replica', scatter_dimension=1, tiled=True)  130 us
    all_to_all x1, blocking collectives, per_device(): lax.all_to_all(back_grad, 'expert', split_axis=0, concat_axis=0, tiled=True)  36.5 us
    all_to_all x1, blocking collectives, per_device(): lax.all_to_all(outgoing_cot, 'expert', split_axis=0, concat_axis=0, tiled...  36.2 us
    unnamed x1, blocking collectives  35 us
    all_gather x1, blocking collectives, per_device(): lax.all_gather(expert_ids[0], 'expert', axis=0, tiled=True)  33.5 us
    all_to_all x1, waiting for transfers between devices, per_device(): lax.all_to_all(back_rows, 'expert', split_axis=0, concat_axis=0, tiled=True)  32.5 us
    all_to_all x1, waiting for transfers between devices, per_device(): lax.all_to_all(outgoing, 'expert', split_axis=0, concat_axis=0, tiled=True)  15.3 us
  transfers between devices with their start and end apart: 4, of which 4 were waited for; matrix products, arithmetic and copies ran while one was open for 6% of the time, Pallas kernels for 0%

commit v1 on v0

v1 whole, which is shorter than its diff:
```python
import jax
import jax.numpy as jnp
from jax import lax
from jax.experimental import pallas as pl
from jax.experimental.pallas import tpu as pltpu
from jax.sharding import PartitionSpec as P

D = 1024
FF = 2048
TOK = 128
CAP = 192
NE = 24
NY = 8
NX = 4
MOST = 10
PACK = 640
ROWS = NE * MOST
PAD = 256
BLK = FF // NY
BF = jnp.bfloat16
F32 = jnp.float32
I32 = jnp.int32
MESH = pl.DeviceIdType.MESH

ORDER = (4, 3, -3, 2, -2, 1, -1, 0)
IDX = {o: i for i, o in enumerate(ORDER)}
IDX[-4] = 0
SIGN = (1, -1)


def nn(a, b):
    return jnp.dot(a, b, preferred_element_type=F32)


def nt(a, b):
    return lax.dot_general(a, b, (((1,), (1,)), ((), ())), preferred_element_type=F32)


def tn(a, b):
    return lax.dot_general(a, b, (((0,), (0,)), ((), ())), preferred_element_type=F32)


def iota(shape, dim):
    return lax.broadcasted_iota(I32, shape, dim)


def div10(v):
    return (v * 6554) >> 16


def div5(v):
    return (v * 13108) >> 16


class Ring:
    def __init__(self, n, own, buf, ssem, rsem, peers, way):
        self.h = n // 2
        self.own, self.buf, self.ssem, self.rsem = own, buf, ssem, rsem
        self.peers, self.way = peers, way
        self.sent = []

    def copy(self, d, s, sub, src):
        return pltpu.make_async_remote_copy(
            src_ref=src,
            dst_ref=self.buf(d, s, sub),
            send_sem=self.ssem(d, s, sub),
            recv_sem=self.rsem(d, s, sub),
            device_id=self.peers[d],
            device_id_type=MESH,
        )

    def arrives(self, d, s, sub):
        return s >= 1 or self.way(sub) == d

    def send(self, d, s, sub):
        mine = self.own(SIGN[d] * (self.h - s), sub)
        src = mine
        if s >= 1 and self.arrives(d, s - 1, sub):
            src = self.buf(d, s - 1, sub)
            self.copy(d, s - 1, sub, src).wait_recv()
            src[...] = src[...] + mine[...]
        out = self.copy(d, s, sub, src)
        out.start()
        self.sent.append(out)

    def last(self, sub):
        total = self.own(0, sub)[...].astype(F32)
        for d in (0, 1):
            if self.arrives(d, self.h - 1, sub):
                got = self.buf(d, self.h - 1, sub)
                self.copy(d, self.h - 1, sub, got).wait_recv()
                total = total + got[...].astype(F32)
        return total

    def drain(self):
        for out in self.sent:
            out.wait_send()


def kernel(
    ids_c, ids_r, count, gate_r, tok_hbm, cot_hbm, w_in_hbm, w_out_hbm,
    mixed, tgrad, gwin, gwout,
    tok, cot, wi, wo, code_s, code_r, out_s, out_r, back_s, back_r, at,
    xs, us, proj, ig, ti, to, z1, z2,
    yr, xr, y2r, x2r,
    lsem, csem, asem, bsem, ys, yv, xsd, xv, y2s, y2v, x2s, x2v,
):
    rep = lax.axis_index("replica")
    me = lax.axis_index("expert")
    py = rep // NX
    px = rep % NX
    y_peers = [{"replica": ((py + g) % NY) * NX + px} for g in (1, NY - 1)]
    x_peers = [{"replica": py * NX + (px + g) % NX} for g in (1, NX - 1)]

    loads = [
        pltpu.make_async_copy(tok_hbm, tok, lsem.at[0]),
        pltpu.make_async_copy(cot_hbm, cot, lsem.at[1]),
    ]
    for i, o in enumerate(ORDER):
        b = (py + (o + NY)) % NY
        at_b = pl.ds(pl.multiple_of(b * BLK, BLK), BLK)
        loads.append(pltpu.make_async_copy(w_in_hbm.at[:, at_b], wi.at[i], lsem.at[2 + i]))
        loads.append(pltpu.make_async_copy(w_out_hbm.at[at_b, :], wo.at[i], lsem.at[10 + i]))
    for load in loads:
        load.start()

    barrier = pltpu.get_barrier_semaphore()

    @pl.loop(1, NE)
    def _(k):
        pl.semaphore_signal(
            barrier, inc=1, device_id={"expert": (me + k) % NE}, device_id_type=MESH
        )

    for peer in y_peers + x_peers:
        pl.semaphore_signal(barrier, inc=1, device_id=peer, device_id_type=MESH)

    n_live = count[...]
    live_c = iota((CAP, 1), 0) < n_live
    live_r = iota((1, CAP), 1) < n_live
    block_c = jnp.where(live_c, ids_c[...] >> 7, NE)
    block_r = ids_r[...] >> 7
    in_block = (block_c == iota((CAP, NE), 1)).astype(F32).astype(BF)
    in_place = ((ids_c[...] & (TOK - 1)) == iota((CAP, TOK), 1)).astype(F32).astype(BF)
    present = tn(in_block, in_place)
    before_me = (iota((TOK, TOK), 0) < iota((TOK, TOK), 1)).astype(F32).astype(BF)
    code = present * (nn(present.astype(BF), before_me) + 1.0)
    code_s[...] = jnp.broadcast_to(code[:, None, :], (NE, 16, TOK)).astype(BF)
    starts = jnp.sum((block_c < block_r).astype(I32), axis=0, keepdims=True)
    spot = MOST * block_r + iota((1, CAP), 1) - starts
    hit = (iota((PAD, CAP), 0) == spot) & live_r
    gate = jnp.sum(jnp.where(hit, gate_r[...], 0.0), axis=1, keepdims=True)

    pl.semaphore_wait(barrier, NE - 1 + 4)

    def scatter(src, dst, ssem, rsem):
        dst[pl.ds(me, 1)] = src[pl.ds(me, 1)]

        @pl.loop(0, NE - 1)
        def _(i):
            k = NE // 2 + ((i + 1) // 2) * (2 * (i % 2) - 1)
            to_e = (me + k) % NE
            pltpu.make_async_remote_copy(
                src_ref=src.at[to_e],
                dst_ref=dst.at[me],
                send_sem=ssem,
                recv_sem=rsem,
                device_id={"expert": to_e},
                device_id_type=MESH,
            ).start()

    def whole(ref, sem):
        part = ref.at[pl.ds(0, NE - 1)]
        pltpu.make_async_copy(part, part, sem).wait()

    scatter(code_s, code_r, csem.at[0], csem.at[1])
    loads[0].wait()
    loads[1].wait()
    whole(code_r, csem.at[1])

    row = iota((NE * 16, TOK), 0) & 15
    kind = jnp.where(row < MOST, 0, 1 + ((row - MOST) >> 1))
    coded = code_r[...].reshape(NE * 16, TOK).astype(F32)

    def chosen(q):
        wanted = jnp.where(row < MOST, row, ((row - MOST) & 1) * 5 + q) + 1
        return (coded == wanted.astype(F32)).astype(F32)

    def by_kind(v, kinds):
        out = v[:, : 128]
        for k in (1, 2, 3):
            out = jnp.where(kinds == k, v[:, k * 128 : (k + 1) * 128], out)
        return out

    for a, rows in enumerate((tok, cot)):
        for q in range(5):
            ahead = jnp.concatenate(
                [rows[:, q * 128 : (q + 1) * 128], rows[:, PACK:]], axis=1
            )
            picked = by_kind(nn(chosen(q).astype(BF), ahead), kind).astype(BF)
            out_s[a, :, :, q * 128 : (q + 1) * 128] = picked.reshape(NE, 16, 128)
        scatter(out_s.at[a], out_r.at[a], asem.at[0, a], asem.at[1, a])

    for q in range(5):
        one = chosen(q)
        for k in range(4):
            at[q, k * 128 : (k + 1) * 128, :] = jnp.where(kind == k, one, 0.0).T.astype(BF)

    gr = iota((80, 128), 0)
    gc = iota((80, 128), 1)
    g_src = div10(gr)
    g_j = gr - MOST * g_src
    g_five = div5(g_j)
    g_q = g_j - 5 * g_five
    same = (gc >> 4) == g_src
    spread = jnp.concatenate(
        [(same & ((gc & 15) == g_j)).astype(F32)]
        + [(same & ((gc & 15) == MOST + 2 * k + g_five)).astype(F32) for k in range(3)],
        axis=0,
    ).astype(BF)

    def unpack(a, put):
        for g in range(3):
            block = out_r[a, g * 8 : (g + 1) * 8].reshape(128, PACK)
            z = nn(spread, block)
            put(g, 0, z[:80])
            for k in range(3):
                zk = z[80 * (k + 1) : 80 * (k + 2)]
                v = zk[:, :128]
                for q in range(1, 5):
                    v = jnp.where(g_q == q, zk[:, q * 128 : (q + 1) * 128], v)
                put(g, PACK + k * 128, v)

    xs[ROWS:] = jnp.zeros((PAD - ROWS, D), BF)
    us[ROWS:] = jnp.zeros((PAD - ROWS, D), BF)

    def put_x(g, c, v):
        xs[g * 80 : (g + 1) * 80, c : c + v.shape[1]] = v.astype(BF)

    def put_u(g, c, v):
        us[g * 80 : (g + 1) * 80, c : c + v.shape[1]] = (
            gate[g * 80 : (g + 1) * 80] * v
        ).astype(BF)

    whole(out_r.at[0], asem.at[1, 0])
    unpack(0, put_x)
    whole(out_r.at[1], asem.at[1, 1])
    unpack(1, put_u)

    half_y = (pl.ds(0, NY // 2), pl.ds(NY // 2, NY // 2))
    flow_y = Ring(
        NY,
        lambda o, c: to.at[IDX[o], c],
        lambda d, s, c: yr.at[d, s, c],
        lambda d, s, c: ys.at[d, s, c],
        lambda d, s, c: yv.at[d, s, c],
        y_peers,
        lambda c: c // 2,
    )
    flow_x = Ring(
        NX,
        lambda o, sub: ti.at[sub[0], (px + (o + NX)) % NX, half_y[sub[1]]],
        lambda d, s, sub: xr.at[d, s, sub[0], sub[1]],
        lambda d, s, sub: xsd.at[d, s, sub[0], sub[1]],
        lambda d, s, sub: xv.at[d, s, sub[0], sub[1]],
        x_peers,
        lambda sub: sub[1],
    )
    flow_y2 = Ring(
        NY,
        lambda o, p: z1.at[(py + (o + NY)) % NY, half_y[p]],
        lambda d, s, p: y2r.at[d, s, p],
        lambda d, s, p: y2s.at[d, s, p],
        lambda d, s, p: y2v.at[d, s, p],
        y_peers,
        lambda p: p,
    )
    flow_x2 = Ring(
        NX,
        lambda o, p: z2.at[(px + (o + NX)) % NX, p],
        lambda d, s, p: x2r.at[d, s, p],
        lambda d, s, p: x2s.at[d, s, p],
        lambda d, s, p: x2v.at[d, s, p],
        x_peers,
        lambda p: p,
    )

    x_all = xs[...]
    u_all = us[...]
    for i, o in enumerate(ORDER):
        loads[2 + 2 * i].wait()
        loads[3 + 2 * i].wait()
        before = nn(x_all, wi[i])
        bell = 0.5 * (1.0 + lax.erf(before * 0.7071067811865476))
        hidden = (before * bell).astype(BF)
        slope = bell + before * jnp.exp(-0.5 * before * before) * 0.3989422804014327
        to[i] = tn(hidden, u_all).astype(BF).reshape(NX, 64, D)
        if o == 4:
            for c in range(NX):
                flow_y.send(c // 2, 0, c)
        if o == 3:
            for c in (2, 3):
                flow_y.send(0, 1, c)
        if o == -3:
            for c in (0, 1):
                flow_y.send(1, 1, c)
        grad = (nt(u_all, wo[i]) * slope).astype(BF)
        term = tn(x_all, grad).astype(BF).reshape(NY, NX, 32, BLK)
        for x in range(NX):
            ti[i, x] = term[:, x]
        for d in (0, 1):
            flow_x.send(d, 0, (i, d))
        for d in (0, 1):
            flow_x.send(d, 1, (i, 1 - d))
        if i == 0:
            proj[...] = nn(hidden, wo[i])
            ig[...] = nt(grad, wi[i])
        else:
            proj[...] += nn(hidden, wo[i])
            ig[...] += nt(grad, wi[i])
        if i == 4:
            for c in (0, 1):
                flow_y.send(0, 1, c)
                flow_y.send(1, 1, c + 2)

    hr = iota((128, 80), 0)
    hc = iota((128, 80), 1)
    h_row = hr & 15
    h_src = div10(hc)
    h_j = hc - MOST * h_src
    h_same = (hr >> 4) == h_src
    h_kind = kind[:128]
    for a, rows in enumerate((proj, ig)):
        for g in range(3):
            part = rows[g * 80 : (g + 1) * 80]
            if a == 0:
                part = gate[g * 80 : (g + 1) * 80] * part
            part = part.astype(BF)
            for q in range(5):
                wanted = jnp.where(h_row < MOST, h_row, ((h_row - MOST) & 1) * 5 + q)
                fold = (h_same & (h_j == wanted)).astype(F32).astype(BF)
                ahead = jnp.concatenate(
                    [part[:, q * 128 : (q + 1) * 128], part[:, PACK:]], axis=1
                )
                back_s[a, g * 8 : (g + 1) * 8, :, q * 128 : (q + 1) * 128] = (
                    by_kind(nn(fold, ahead), h_kind).astype(BF).reshape(8, 16, 128)
                )
        scatter(back_s.at[a], back_r.at[a], bsem.at[0, a], bsem.at[1, a])

    ways = [(d, c) for c in (2, 3, 0, 1) for d in (0, 1)]
    ways = [(d, c if d == 0 else (c + 2) % 4) for d, c in ways]
    for i in range(NY):
        d, c = ways[i]
        flow_y.send(d, 2, c)
        flow_x.send(0, 1, (i, 0))
        flow_x.send(1, 1, (i, 1))
    for i, o in enumerate(ORDER):
        d, c = ways[i]
        flow_y.send(d, 3, c)
        b = (py + (o + NY)) % NY
        for p in (0, 1):
            z1[half_y[p], pl.ds(b, 1)] = flow_x.last((i, p)).astype(BF)[:, None]
    for d in (0, 1):
        flow_y2.send(d, 0, d)
    for d in (0, 1):
        flow_y2.send(d, 1, 1 - d)
    for c in range(NX):
        z2[c] = flow_y.last(c).astype(BF).reshape(2, 32, D)
    for d in (0, 1):
        flow_x2.send(d, 0, d)
    for d in (0, 1):
        flow_x2.send(d, 1, 1 - d)
    for d in (0, 1):
        flow_y2.send(d, 1, d)
    for d in (0, 1):
        flow_x2.send(d, 1, d)
    for p in (0, 1):
        for d in (0, 1):
            flow_y2.send(d, 2, (1 - d + p) % 2)

    for a, dest in enumerate((mixed, tgrad)):
        whole(back_r.at[a], bsem.at[1, a])
        tail = [jnp.zeros((TOK, 128), F32) for _ in range(3)]
        for q in range(5):
            z = nn(at[q], back_r[a, :, :, q * 128 : (q + 1) * 128].reshape(NE * 16, 128))
            dest[:, q * 128 : (q + 1) * 128] = z[:128].astype(BF)
            for k in range(3):
                tail[k] = tail[k] + z[(k + 1) * 128 : (k + 2) * 128]
        for k in range(3):
            dest[:, PACK + k * 128 : PACK + (k + 1) * 128] = tail[k].astype(BF)

    for p in (0, 1):
        for d in (0, 1):
            flow_y2.send(d, 3, (1 - d + p) % 2)
    scale = 1.0 / (NX * NY)
    for p in (0, 1):
        gwout[p * 32 : (p + 1) * 32] = (flow_x2.last(p) * scale).astype(BF)
    for p in (0, 1):
        total = (flow_y2.last(p) * scale).astype(BF)
        for b in range(NY // 2):
            at_b = (p * (NY // 2) + b) * BLK
            gwin[:, at_b : at_b + BLK] = total[b]

    for flow in (flow_y, flow_x, flow_y2, flow_x2):
        flow.drain()
    whole(code_s, csem.at[0])
    for a in (0, 1):
        whole(out_s.at[a], asem.at[0, a])
        whole(back_s.at[a], bsem.at[0, a])


def per_device(tokens, cotangent, w_in, w_out, gate_values, expert_ids, valid_counts):
    vm = pl.BlockSpec(memory_space=pltpu.VMEM)
    hbm = pl.BlockSpec(memory_space=pl.ANY)
    dma = pltpu.SemaphoreType.DMA
    blocks = (2, NE, 16, PACK)
    mixed, tgrad, gwin, gwout = pl.pallas_call(
        kernel,
        out_shape=(
            jax.ShapeDtypeStruct((TOK, D), BF),
            jax.ShapeDtypeStruct((TOK, D), BF),
            jax.ShapeDtypeStruct((32, FF), BF),
            jax.ShapeDtypeStruct((64, D), BF),
        ),
        in_specs=[vm] * 4 + [hbm] * 4,
        out_specs=(vm,) * 4,
        scratch_shapes=[
            pltpu.VMEM((TOK, D), BF),
            pltpu.VMEM((TOK, D), BF),
            pltpu.VMEM((NY, D, BLK), BF),
            pltpu.VMEM((NY, BLK, D), BF),
            pltpu.VMEM((NE, 16, TOK), BF),
            pltpu.VMEM((NE, 16, TOK), BF),
            pltpu.VMEM(blocks, BF),
            pltpu.VMEM(blocks, BF),
            pltpu.VMEM(blocks, BF),
            pltpu.VMEM(blocks, BF),
            pltpu.VMEM((5, 512, NE * 16), BF),
            pltpu.VMEM((PAD, D), BF),
            pltpu.VMEM((PAD, D), BF),
            pltpu.VMEM((PAD, D), F32),
            pltpu.VMEM((PAD, D), F32),
            pltpu.VMEM((NY, NX, NY, 32, BLK), BF),
            pltpu.VMEM((NY, NX, 64, D), BF),
            pltpu.VMEM((NY, NY, 32, BLK), BF),
            pltpu.VMEM((NX, 2, 32, D), BF),
            pltpu.VMEM((2, 4, NX, 64, D), BF),
            pltpu.VMEM((2, 2, NY, 2, NY // 2, 32, BLK), BF),
            pltpu.VMEM((2, 4, 2, NY // 2, 32, BLK), BF),
            pltpu.VMEM((2, 2, 2, 32, D), BF),
            dma((18,)),
            dma((2,)),
            dma((2, 2)),
            dma((2, 2)),
            dma((2, 4, NX)),
            dma((2, 4, NX)),
            dma((2, 2, NY, 2)),
            dma((2, 2, NY, 2)),
            dma((2, 4, 2)),
            dma((2, 4, 2)),
            dma((2, 2, 2)),
            dma((2, 2, 2)),
        ],
        compiler_params=pltpu.CompilerParams(
            collective_id=0, has_side_effects=True, vmem_limit_bytes=56 * 1024 * 1024
        ),
        cost_estimate=pl.CostEstimate(
            flops=12 * PAD * D * FF, bytes_accessed=10 * 1024 * 1024, transcendentals=2 * PAD * FF
        ),
    )(
        expert_ids.reshape(CAP, 1),
        expert_ids.reshape(1, CAP),
        valid_counts,
        gate_values.reshape(1, CAP),
        tokens[0],
        cotangent[0],
        w_in[0],
        w_out[0],
    )
    return mixed[None], tgrad[None], gwin[None], gwout[None]


def solution(mesh):
    placed = (
        P("replica", "expert", None),
        P("replica", "expert", None),
        P("expert", None, None),
        P("expert", None, None),
        P("replica", "expert", None),
        P("replica", "expert", None),
        P("replica", "expert"),
    )
    return jax.shard_map(
        per_device,
        mesh=mesh,
        in_specs=placed,
        out_specs=(
            P("replica", "expert", None),
            P("replica", "expert", None),
            P("expert", "replica", None),
            P("expert", "replica", None),
        ),
        check_vma=False,
    )
```

time: 641 us -> 131 us (0.20)
  waiting for transfers between devices: 413 us -> 0 us
  blocking collectives: 141 us -> 0 us
  Pallas kernels: 0 us -> 121 us
  matrix products: 22.8 us -> 0 us
  other arithmetic: 21.8 us -> 0 us
  between operations: 15 us -> 1.29 us
  local copies, waits for them, and re-layouts: 18.3 us -> 7.92 us
  starting transfers between devices: 8.05 us -> 0 us
    reduce_scatter x2 -> x0, waiting for transfers between devices: 365 us -> none  [the longest x1 235 us: per_device(): lax.psum_scatter(term_in[None], 'replica', scatter_dimension=1, tiled=True)]
    pallas_call x0 -> x1, Pallas kernels: none -> 121 us  [per_device(): pl.pallas_call(kernel, out_shape=(jax.ShapeDtypeStruct((TOK, D), BF), jax...]
    all_to_all x2 -> x0, blocking collectives: 72.7 us -> none  [the longest x1 36.5 us: per_device(): lax.all_to_all(back_grad, 'expert', split_axis=0, concat_axis=0, tiled=True)]
    all_to_all x2 -> x0, waiting for transfers between devices: 47.8 us -> none  [the longest x1 32.5 us: per_device(): lax.all_to_all(back_rows, 'expert', split_axis=0, concat_axis=0, tiled=True)]
    unnamed x1 -> x0, blocking collectives: 35 us -> none
    all_gather x1 -> x0, blocking collectives: 33.5 us -> none  [per_device(): lax.all_gather(expert_ids[0], 'expert', axis=0, tiled=True)]
    dot_general x8 -> x0, matrix products: 22.8 us -> none  [the longest x2 7.72 us: contract_cols(): lax.dot_general(left, right, (((1,), (1,)), ((), ())), preferred_element_...]
    gather x7 -> x0, other arithmetic: 15.1 us -> none  [the longest x3 15 us: per_device(): own_starts[own_source]]
  transfers between devices with their start and end apart: 4 -> 0, of which waited for: 4 -> 0; matrix products, arithmetic and copies ran while one was open for 6% -> 0% of each run, Pallas kernels for 0% -> 0%
where the time goes in v1:
time: 131 us; the launch traced here: 130 us
  Pallas kernels  121 us (92%)
  local copies, waits for them, and re-layouts  7.92 us (6%)
    pallas_call x1, Pallas kernels, per_device(): pl.pallas_call(kernel, out_shape=(jax.ShapeDtypeStruct((TOK, D), BF), jax...  121 us
    unnamed x4, local copies, waits for them, and re-layouts  6.47 us

profile of v1, /device:TPU:16, one launch (start us, length us, event | category | flops | bytes accessed | tf_op | source)
XLA Modules:
  0.0 130.3 jit_solution(4572215911148429760)
XLA Ops:
  1.3 1.4 %copy.11.ids_c = s32[192,1]{1,0:T(8,128)} copy(s32[192,1]{0,1:T(1,128)} %bitcast.15) | data formatting | bytes 1536 | tf_op jit(solution)/shard_map/reshape | solution.py:471
  2.7 121.1 %shard_map.102 = (bf16[128,1024]{1,0:T(8,128)(2,1)}, bf16[128,1024]{1,0:T(8,128)(2,1)}, bf16[32,2048]{1,0:T(8,128)(2,1)}, bf16[64,1024]{1,0:T(8,128)(2,1)}) custom-call(s32[192,1]{1,0:T(8,128)} %copy.11.ids_c, s32[1,192]{1,0:T(1,128)} %bitcast.16, s32[1,1]{1,0:T(1,128)S(6)} %copy.16.count, f32[1,192]{1,0:T(1,128)} %bitcast.21, bf16[128,1024]{1,0:T(8,128)(2,1)} %bitcast.19, ...), custom_call_target="tpu_custom_call" | custom-call | flops 6442450944 | bytes 10485760 | tf_op jit(solution)/shard_map/pallas_call | solution.py:417
  123.8 1.7 %copy.17 = bf16[1,128,1024]{2,1,0:T(8,128)(2,1)} copy(bf16[1,128,1024]{2,1,0:T(8,128)(2,1)} %bitcast.12) | data formatting | bytes 524288
  125.5 1.7 %copy.18 = bf16[1,128,1024]{2,1,0:T(8,128)(2,1)} copy(bf16[1,128,1024]{2,1,0:T(8,128)(2,1)} %bitcast.11) | data formatting | bytes 524288
  127.2 1.6 %copy.19 = bf16[1,32,2048]{2,1,0:T(8,128)(2,1)} copy(bf16[1,32,2048]{2,1,0:T(8,128)(2,1)} %bitcast.14) | data formatting | bytes 262144
  128.7 1.6 %copy.20 = bf16[1,64,1024]{2,1,0:T(8,128)(2,1)} copy(bf16[1,64,1024]{2,1,0:T(8,128)(2,1)} %bitcast.13) | data formatting | bytes 262144

commit v2 on v1

v2 whole, which is shorter than its diff:
```python
import jax
import jax.numpy as jnp
from jax import lax
from jax.experimental import pallas as pl
from jax.experimental.pallas import tpu as pltpu
from jax.sharding import PartitionSpec as P

D = 1024
FF = 2048
TOK = 128
CAP = 192
NE = 24
NY = 8
NX = 4
MOST = 10
NQ = 5
NC = D // 128
COLS = tuple(tuple(range(16 * q // MOST, (16 * q + 15) // MOST + 1)) for q in range(NQ))
EARLY = 384
E_TILES = 2
ROWS = NE * MOST
PAD = 256
BLK = FF // NY
BF = jnp.bfloat16
F32 = jnp.float32
I32 = jnp.int32
MESH = pl.DeviceIdType.MESH

ORDER = (4, 3, -3, 2, -2, 1, -1, 0)
IDX = {o: i for i, o in enumerate(ORDER)}
IDX[-4] = 0
SIGN = (1, -1)


def nn(a, b):
    return jnp.dot(a, b, preferred_element_type=F32)


def nt(a, b):
    return lax.dot_general(a, b, (((1,), (1,)), ((), ())), preferred_element_type=F32)


def tn(a, b):
    return lax.dot_general(a, b, (((0,), (0,)), ((), ())), preferred_element_type=F32)


def iota(shape, dim):
    return lax.broadcasted_iota(I32, shape, dim)


def div10(v):
    return (v * 6554) >> 16


PLAN = (
    ("toe", 0), ("e", 0, 0, 0), ("e", 1, 0, 1), ("proj",), ("toe", 1), ("toe", 2), ("e", 0, 1, 1),
    ("e", 1, 1, 0), ("toe", 3), ("toe", 4), ("toe", 5), ("toe", 6), ("e", 0, 1, 0), ("e", 1, 1, 1),
    ("toe", 7), ("e", 0, 2, 1), ("e", 1, 2, 0), ("e", 0, 2, 0), ("e", 1, 2, 1), ("cb",), ("ti", 0),
    ("x", 0, 0, (0, 0)), ("x", 1, 0, (0, 1)), ("x", 0, 1, (0, 1)), ("x", 1, 1, (0, 0)), ("tol", 0),
    ("y", 0, 0, 0), ("y", 0, 0, 1), ("y", 1, 0, 2), ("y", 1, 0, 3), ("ti", 1), ("x", 0, 0, (1, 0)),
    ("x", 1, 0, (1, 1)), ("x", 0, 1, (1, 1)), ("x", 1, 1, (1, 0)), ("ti", 2), ("x", 0, 0, (2, 0)),
    ("x", 1, 0, (2, 1)), ("x", 0, 1, (2, 1)), ("x", 1, 1, (2, 0)), ("x", 0, 1, (0, 0)),
    ("x", 1, 1, (0, 1)), ("tol", 1), ("y", 0, 1, 0), ("y", 0, 1, 2), ("y", 0, 1, 3), ("tol", 2),
    ("y", 1, 1, 2), ("y", 1, 1, 0), ("y", 1, 1, 1), ("ti", 3), ("y", 0, 1, 1), ("y", 1, 1, 3),
    ("x", 0, 0, (3, 0)), ("x", 1, 0, (3, 1)), ("x", 0, 1, (1, 0)), ("x", 1, 1, (1, 1)),
    ("x", 0, 1, (3, 1)), ("x", 1, 1, (3, 0)), ("ti", 4), ("x", 0, 0, (4, 0)), ("x", 1, 0, (4, 1)),
    ("tol", 3), ("y", 0, 2, 0), ("x", 0, 1, (2, 0)), ("x", 1, 1, (2, 1)), ("y", 0, 2, 2),
    ("tol", 4), ("y", 1, 2, 0), ("y", 1, 2, 2), ("x", 0, 1, (4, 1)), ("x", 1, 1, (4, 0)), ("ti", 5),
    ("z1", 0), ("y", 0, 2, 3), ("y", 1, 2, 1), ("x", 0, 0, (5, 0)), ("x", 1, 0, (5, 1)),
    ("x", 0, 1, (3, 0)), ("y", 0, 2, 1), ("x", 1, 1, (3, 1)), ("y", 1, 2, 3), ("x", 0, 1, (5, 1)),
    ("x", 1, 1, (5, 0)), ("z1", 1), ("y2", 0, 0, 0), ("tol", 5), ("y2", 1, 1, 0), ("tol", 6),
    ("ti", 6), ("x", 0, 0, (6, 0)), ("x", 1, 0, (6, 1)), ("x", 0, 1, (6, 1)), ("x", 1, 1, (6, 0)),
    ("e", 0, 3, 0), ("e", 1, 3, 0), ("x", 0, 1, (4, 0)), ("x", 1, 1, (4, 1)), ("e", 0, 3, 1),
    ("ti", 7), ("z1", 2), ("x", 0, 0, (7, 0)), ("x", 1, 0, (7, 1)), ("packg",), ("y2", 0, 1, 0),
    ("x", 0, 1, (5, 0)), ("x", 1, 1, (5, 1)), ("x", 0, 1, (7, 1)), ("x", 1, 1, (7, 0)),
    ("y2", 1, 2, 0), ("e", 1, 3, 1), ("z1", 3), ("y2", 1, 0, 1), ("y2", 0, 1, 1), ("y", 0, 3, 0),
    ("y", 0, 3, 1), ("y", 1, 3, 0), ("tol", 7), ("y", 1, 3, 1), ("y", 0, 3, 2), ("y2", 1, 3, 0),
    ("x", 0, 1, (6, 0)), ("x", 1, 1, (6, 1)), ("y2", 0, 2, 0), ("y2", 0, 2, 1), ("y", 1, 3, 2),
    ("y", 0, 3, 3), ("y", 1, 3, 3), ("mixed",), ("z1", 4), ("y2", 1, 1, 1), ("ze", 0), ("ze", 1),
    ("x", 0, 1, (7, 0)), ("x", 1, 1, (7, 1)), ("zl", 0), ("z1", 5), ("y2", 0, 0, 2),
    ("y2", 1, 1, 2), ("zl", 1), ("y2", 0, 3, 0), ("y2", 0, 3, 1), ("zl", 2), ("z1", 6), ("z1", 7),
    ("y2", 1, 0, 3), ("y2", 0, 1, 2), ("y2", 0, 1, 3), ("zl", 3), ("x2", 0, 0, 0), ("x2", 1, 0, 1),
    ("y2", 1, 2, 1), ("x2", 0, 1, 1), ("y2", 1, 2, 2), ("x2", 1, 1, 0), ("fi", 0), ("y2", 1, 1, 3),
    ("y2", 0, 2, 2), ("y2", 0, 2, 3), ("tgrad",), ("x2", 0, 1, 0), ("y2", 1, 2, 3), ("x2", 1, 1, 1),
    ("y2", 0, 3, 2), ("y2", 1, 3, 1), ("y2", 0, 3, 3), ("y2", 1, 3, 2), ("y2", 1, 3, 3), ("fo", 0),
    ("fi", 1), ("fo", 1), ("fi", 2), ("fi", 3),
)


class Ring:
    def __init__(self, n, own, buf, ssem, rsem, peers, way):
        self.h = n // 2
        self.own, self.buf, self.ssem, self.rsem = own, buf, ssem, rsem
        self.peers, self.way = peers, way
        self.sent = []

    def copy(self, d, s, sub, src):
        return pltpu.make_async_remote_copy(
            src_ref=src,
            dst_ref=self.buf(d, s, sub),
            send_sem=self.ssem(d, s, sub),
            recv_sem=self.rsem(d, s, sub),
            device_id=self.peers[d],
            device_id_type=MESH,
        )

    def arrives(self, d, s, sub):
        return s >= 1 or self.way(sub) == d

    def send(self, d, s, sub):
        mine = self.own(SIGN[d] * (self.h - s), sub)
        src = mine
        if s >= 1 and self.arrives(d, s - 1, sub):
            src = self.buf(d, s - 1, sub)
            self.copy(d, s - 1, sub, src).wait_recv()
            src[...] = src[...] + mine[...]
        out = self.copy(d, s, sub, src)
        out.start()
        self.sent.append(out)

    def last(self, sub):
        total = self.own(0, sub)[...].astype(F32)
        for d in (0, 1):
            if self.arrives(d, self.h - 1, sub):
                got = self.buf(d, self.h - 1, sub)
                self.copy(d, self.h - 1, sub, got).wait_recv()
                total = total + got[...].astype(F32)
        return total

    def drain(self):
        for out in self.sent:
            out.wait_send()


def kernel(
    ids_r, count, gate_r, tok_hbm, cot_hbm, w_in_hbm, w_out_hbm,
    mixed, tgrad, gwin, gwout,
    tok, cot, wi, wo, code_s, code_r, out_s, out_r, back_s, back_r, at,
    xs, xt, us, hid, hid_t, slopes, proj, ig, ti, toe, tol, z1, z2,
    yer, yr, xr, y2r, x2r,
    lsem, csem, asem, bsem, yes, yev, ys, yv, xsd, xv, y2s, y2v, x2s, x2v,
):
    rep = lax.axis_index("replica")
    me = lax.axis_index("expert")
    py = rep // NX
    px = rep % NX
    y_peers = [{"replica": ((py + g) % NY) * NX + px} for g in (1, NY - 1)]
    x_peers = [{"replica": py * NX + (px + g) % NX} for g in (1, NX - 1)]

    barrier = pltpu.get_barrier_semaphore()

    @pl.loop(1, NE)
    def _(k):
        pl.semaphore_signal(
            barrier, inc=1, device_id={"expert": (me + k) % NE}, device_id_type=MESH
        )

    for peer in y_peers + x_peers:
        pl.semaphore_signal(barrier, inc=1, device_id=peer, device_id_type=MESH)

    loads = [
        pltpu.make_async_copy(here, there, lsem.at[n])
        for n, (here, there) in enumerate(
            ((tok_hbm, tok), (cot_hbm, cot), (w_in_hbm, wi), (w_out_hbm, wo))
        )
    ]
    for load in loads:
        load.start()

    n_live = count[...]
    row_ids = ids_r[...]
    col_ids = jnp.broadcast_to(row_ids.astype(F32), (8, CAP)).T[:, :1].astype(I32)
    live_c = iota((CAP, 1), 0) < n_live
    live_r = iota((1, CAP), 1) < n_live
    block_c = jnp.where(live_c, col_ids >> 7, NE)
    block_r = row_ids >> 7
    in_block = (block_c == iota((CAP, NE), 1)).astype(F32).astype(BF)
    in_place = ((col_ids & (TOK - 1)) == iota((CAP, TOK), 1)).astype(F32).astype(BF)
    present = tn(in_block, in_place)
    before_me = (iota((TOK, TOK), 0) < iota((TOK, TOK), 1)).astype(F32).astype(BF)
    code = present * (nn(present.astype(BF), before_me) + 1.0)
    code_s[...] = jnp.broadcast_to(code[:, None, :], (NE, 16, TOK)).astype(BF)

    pl.semaphore_wait(barrier, NE - 1 + 4)

    def scatter(src, dst, ssem, rsem, part=None):
        def cut(ref, e):
            return ref.at[e] if part is None else ref.at[e, part]

        @pl.loop(0, NE - 1)
        def _(i):
            k = NE // 2 + ((i + 1) // 2) * (2 * (i % 2) - 1)
            to_e = (me + k) % NE
            pltpu.make_async_remote_copy(
                src_ref=cut(src, to_e),
                dst_ref=cut(dst, me),
                send_sem=ssem,
                recv_sem=rsem,
                device_id={"expert": to_e},
                device_id_type=MESH,
            ).start()

        if part is None:
            dst[pl.ds(me, 1)] = src[pl.ds(me, 1)]
        else:
            dst[pl.ds(me, 1), part] = src[pl.ds(me, 1), part]

    def whole(ref, sem, part=None):
        got = ref.at[pl.ds(0, NE - 1)] if part is None else ref.at[pl.ds(0, NE - 1), part]
        pltpu.make_async_copy(got, got, sem).wait()

    scatter(code_s, code_r, csem.at[0], csem.at[1])
    starts = jnp.sum((block_c < block_r).astype(I32), axis=0, keepdims=True)
    spot = MOST * block_r + iota((1, CAP), 1) - starts
    hit = (iota((PAD, CAP), 0) == spot) & live_r
    gate = jnp.sum(jnp.where(hit, gate_r[...], 0.0), axis=1, keepdims=True)
    loads[0].wait()
    loads[1].wait()
    whole(code_r, csem.at[1])

    row = iota((NE * 16, TOK), 0) & 15
    coded = code_r[...].reshape(NE * 16, TOK).astype(F32)

    def chosen(q):
        n = row + 16 * q
        return (coded == (n - MOST * div10(n) + 1).astype(F32)).astype(F32)

    def by_block(v, q, rows):
        block = div10(rows + 16 * q)
        out = v[:, :128]
        for k in range(1, len(COLS[q])):
            out = jnp.where(block == COLS[q][k], v[:, k * 128 : (k + 1) * 128], out)
        return out.astype(BF)

    def columns(q):
        return slice(COLS[q][0] * 128, (COLS[q][-1] + 1) * 128)

    def fill(a, rows):
        for q in range(NQ):
            v = nn(chosen(q).astype(BF), rows[:, columns(q)])
            out_s[a, :, q] = by_block(v, q, row).reshape(NE, 16, 128)

    first, second = pl.ds(0, E_TILES), pl.ds(E_TILES, NQ - E_TILES)
    fill(0, tok)
    scatter(out_s.at[0], out_r.at[0], asem.at[0, 0], asem.at[1, 0])
    fill(1, cot)
    scatter(out_s.at[1], out_r.at[1], asem.at[0, 1], asem.at[1, 1], first)

    for q in range(NQ):
        one = chosen(q)
        block = div10(row + 16 * q)
        for k, c in enumerate(COLS[q]):
            at[q, k * 128 : (k + 1) * 128, :] = jnp.where(block == c, one, 0.0).T.astype(BF)

    gr = iota((80, 128), 0)
    gc = iota((80, 128), 1)
    g_src = div10(gr)
    same = (gc >> 4) == g_src

    def unpack(a, blocks, put):
        for c in blocks:
            tiles = [q for q in range(NQ) if c in COLS[q]]
            spread = jnp.concatenate(
                [
                    (same & ((gc & 15) + 16 * q == MOST * c + gr - MOST * g_src)).astype(F32)
                    for q in tiles
                ],
                axis=1,
            ).astype(BF)
            came = jnp.concatenate(
                [
                    jnp.concatenate(
                        [out_r[a, g * 8 : (g + 1) * 8, q].reshape(128, 128) for g in range(3)],
                        axis=1,
                    )
                    for q in tiles
                ],
                axis=0,
            )
            v = nn(spread, came)
            for g in range(3):
                put(g, c, v[:, g * 128 : (g + 1) * 128])

    xs[ROWS:] = jnp.zeros((PAD - ROWS, D), BF)
    us[ROWS:] = jnp.zeros((PAD - ROWS, D), BF)

    def put_x(g, c, v):
        xs[g * 80 : (g + 1) * 80, c * 128 : (c + 1) * 128] = v.astype(BF)

    def put_u(g, c, v):
        us[g * 80 : (g + 1) * 80, c * 128 : (c + 1) * 128] = (
            gate[g * 80 : (g + 1) * 80] * v
        ).astype(BF)

    half = (pl.ds(0, NY // 2), pl.ds(NY // 2, NY // 2))
    flow_e = Ring(
        NY,
        lambda o, p: toe.at[IDX[o], pl.ds(2 * p, 2)],
        lambda d, s, p: yer.at[d, s, p],
        lambda d, s, p: yes.at[d, s, p],
        lambda d, s, p: yev.at[d, s, p],
        y_peers,
        lambda p: p,
    )
    flow_y = Ring(
        NY,
        lambda o, c: tol.at[IDX[o], c],
        lambda d, s, c: yr.at[d, s, c],
        lambda d, s, c: ys.at[d, s, c],
        lambda d, s, c: yv.at[d, s, c],
        y_peers,
        lambda c: c // 2,
    )
    flow_x = Ring(
        NX,
        lambda o, sub: ti.at[sub[0], (px + (o + NX)) % NX, half[sub[1]]],
        lambda d, s, sub: xr.at[d, s, sub[0], sub[1]],
        lambda d, s, sub: xsd.at[d, s, sub[0], sub[1]],
        lambda d, s, sub: xv.at[d, s, sub[0], sub[1]],
        x_peers,
        lambda sub: sub[1],
    )
    flow_y2 = Ring(
        NY,
        lambda o, p: z1.at[(py + (o + NY)) % NY, pl.ds(2 * p, 2)],
        lambda d, s, p: y2r.at[d, s, p],
        lambda d, s, p: y2s.at[d, s, p],
        lambda d, s, p: y2v.at[d, s, p],
        y_peers,
        lambda p: p % 2,
    )
    flow_x2 = Ring(
        NX,
        lambda o, p: z2.at[(px + (o + NX)) % NX, p],
        lambda d, s, p: x2r.at[d, s, p],
        lambda d, s, p: x2s.at[d, s, p],
        lambda d, s, p: x2v.at[d, s, p],
        x_peers,
        lambda p: p,
    )

    loads[2].wait()
    loads[3].wait()
    whole(out_r.at[0], asem.at[1, 0])
    scatter(out_s.at[1], out_r.at[1], asem.at[0, 2], asem.at[1, 2], second)
    unpack(0, range(NC), put_x)
    x_all = xs[...]
    for b in range(NY):
        before = nn(x_all, wi[:, b * BLK : (b + 1) * BLK])
        bell = 0.5 * (1.0 + lax.erf(before * 0.7071067811865476))
        hidden = (before * bell).astype(BF)
        hid[b] = hidden
        hid_t[b] = hidden.T
        slopes[b] = bell + before * jnp.exp(-0.5 * before * before) * 0.3989422804014327
    xt[...] = x_all.T

    hr = iota((128, 80), 0)
    hc = iota((128, 80), 1)
    h_src = div10(hc)
    h_same = (hr >> 4) == h_src

    def pack(a, rows):
        for q in range(NQ):
            n = (hr & 15) + 16 * q
            fold = (h_same & (hc - MOST * h_src == n - MOST * div10(n))).astype(F32).astype(BF)
            for g in range(3):
                v = nn(fold, rows(g)[:, columns(q)])
                back_s[a, g * 8 : (g + 1) * 8, q] = by_block(v, q, row[:128]).reshape(8, 16, 128)

    def term_out(i, u, dest):
        o = ORDER[i]
        term = nn(hid_t[(py + (o + NY)) % NY], u)
        dest[i] = term.astype(BF).reshape(NX, 64, u.shape[1])

    def term_in(i):
        grad = (nt(us[...], wo[i]) * slopes[i]).astype(BF)
        term = nn(xt[...], grad).astype(BF).reshape(NY, NX, 32, BLK)
        for x in range(NX):
            ti[i, x] = term[:, x]
        if i == 0:
            ig[...] = nt(grad, wi[:, i * BLK : (i + 1) * BLK])
        else:
            ig[...] += nt(grad, wi[:, i * BLK : (i + 1) * BLK])

    def project():
        for b in range(NY):
            if b == 0:
                proj[...] = nn(hid[b], wo[b])
            else:
                proj[...] += nn(hid[b], wo[b])
        pack(0, lambda g: (gate[g * 80 : (g + 1) * 80] * proj[g * 80 : (g + 1) * 80]).astype(BF))

    def second_cotangents():
        whole(out_r.at[1], asem.at[1, 2], second)
        scatter(back_s.at[0], back_r.at[0], bsem.at[0, 0], bsem.at[1, 0])
        unpack(1, range(EARLY // 128, NC), put_u)

    def input_grads_back():
        pack(1, lambda g: ig[g * 80 : (g + 1) * 80].astype(BF))
        scatter(back_s.at[1], back_r.at[1], bsem.at[0, 1], bsem.at[1, 1])

    def into_z1(i):
        for p in (0, 1):
            z1[half[p], i : i + 1] = flow_x.last((i, p)).astype(BF)[:, None]

    def early_z2(p):
        z2[2 * p : 2 * p + 2, :, :, :EARLY] = (
            flow_e.last(p).astype(BF).reshape(2, 2, 32, EARLY)
        )

    def late_z2(c):
        z2[c, :, :, EARLY:] = flow_y.last(c).astype(BF).reshape(2, 32, D - EARLY)

    def gather(a, dest):
        whole(back_r.at[a], bsem.at[1, a])
        sums = [None] * NC
        for q in range(NQ):
            z = nn(at[q, : len(COLS[q]) * 128], back_r[a, :, q].reshape(NE * 16, 128))
            for k, c in enumerate(COLS[q]):
                part = z[k * 128 : (k + 1) * 128]
                sums[c] = part if sums[c] is None else sums[c] + part
        for c in range(NC):
            dest[:, c * 128 : (c + 1) * 128] = sums[c].astype(BF)

    scale = 1.0 / (NX * NY)

    def finish_in(p):
        total = (flow_y2.last(p) * scale).astype(BF)
        for k in range(2):
            at_b = (2 * p + k) * BLK
            gwin[:, at_b : at_b + BLK] = total[k]

    def finish_out(p):
        gwout[p * 32 : (p + 1) * 32] = (flow_x2.last(p) * scale).astype(BF)

    steps = {
        "e": flow_e.send,
        "y": flow_y.send,
        "x": flow_x.send,
        "y2": flow_y2.send,
        "x2": flow_x2.send,
        "toe": lambda i: term_out(i, us[:, :EARLY], toe),
        "tol": lambda i: term_out(i, us[:, EARLY:], tol),
        "ti": term_in,
        "proj": project,
        "cb": second_cotangents,
        "packg": input_grads_back,
        "z1": into_z1,
        "ze": early_z2,
        "zl": late_z2,
        "mixed": lambda: gather(0, mixed),
        "tgrad": lambda: gather(1, tgrad),
        "fi": finish_in,
        "fo": finish_out,
    }
    whole(out_r.at[1], asem.at[1, 1], first)
    unpack(1, range(EARLY // 128), put_u)
    for name, *at_step in PLAN:
        steps[name](*at_step)

    for flow in (flow_e, flow_y, flow_x, flow_y2, flow_x2):
        flow.drain()
    whole(code_s, csem.at[0])
    whole(out_s.at[0], asem.at[0, 0])
    whole(out_s.at[1], asem.at[0, 1], first)
    whole(out_s.at[1], asem.at[0, 2], second)
    for a in (0, 1):
        whole(back_s.at[a], bsem.at[0, a])


def place(*refs):
    sems = refs[-1]
    made, out, held = refs[:4], refs[4:8], refs[8:12]
    for k in range(4):
        pltpu.make_async_copy(made[k], held[k], sems.at[0, k]).start()
    for k in range(4):
        pltpu.make_async_copy(made[k], held[k], sems.at[0, k]).wait()
        pltpu.make_async_copy(held[k], out[k], sems.at[1, k]).start()
    for k in range(4):
        pltpu.make_async_copy(held[k], out[k], sems.at[1, k]).wait()


def per_device(tokens, cotangent, w_in, w_out, gate_values, expert_ids, valid_counts):
    vm = pl.BlockSpec(memory_space=pltpu.VMEM)
    hbm = pl.BlockSpec(memory_space=pl.ANY)
    dma = pltpu.SemaphoreType.DMA
    blocks = (2, NE, NQ, 16, 128)
    results = (
        jax.ShapeDtypeStruct((TOK, D), BF),
        jax.ShapeDtypeStruct((TOK, D), BF),
        jax.ShapeDtypeStruct((32, FF), BF),
        jax.ShapeDtypeStruct((64, D), BF),
    )
    late = D - EARLY
    made = pl.pallas_call(
        kernel,
        out_shape=results,
        in_specs=[vm] * 3 + [hbm] * 4,
        out_specs=(vm,) * 4,
        scratch_shapes=[
            pltpu.VMEM((TOK, D), BF),
            pltpu.VMEM((TOK, D), BF),
            pltpu.VMEM((D, FF), BF),
            pltpu.VMEM((NY, BLK, D), BF),
            pltpu.VMEM((NE, 16, TOK), BF),
            pltpu.VMEM((NE, 16, TOK), BF),
            pltpu.VMEM(blocks, BF),
            pltpu.VMEM(blocks, BF),
            pltpu.VMEM(blocks, BF),
            pltpu.VMEM(blocks, BF),
            pltpu.VMEM((NQ, 384, NE * 16), BF),
            pltpu.VMEM((PAD, D), BF),
            pltpu.VMEM((D, PAD), BF),
            pltpu.VMEM((PAD, D), BF),
            pltpu.VMEM((NY, PAD, BLK), BF),
            pltpu.VMEM((NY, BLK, PAD), BF),
            pltpu.VMEM((NY, PAD, BLK), F32),
            pltpu.VMEM((PAD, D), F32),
            pltpu.VMEM((PAD, D), F32),
            pltpu.VMEM((NY, NX, NY, 32, BLK), BF),
            pltpu.VMEM((NY, NX, 64, EARLY), BF),
            pltpu.VMEM((NY, NX, 64, late), BF),
            pltpu.VMEM((NY, NY, 32, BLK), BF),
            pltpu.VMEM((NX, 2, 32, D), BF),
            pltpu.VMEM((2, 4, 2, 2, 64, EARLY), BF),
            pltpu.VMEM((2, 4, NX, 64, late), BF),
            pltpu.VMEM((2, 2, NY, 2, NY // 2, 32, BLK), BF),
            pltpu.VMEM((2, 4, 4, 2, 32, BLK), BF),
            pltpu.VMEM((2, 2, 2, 32, D), BF),
            dma((4,)),
            dma((2,)),
            dma((2, 3)),
            dma((2, 2)),
            dma((2, 4, 2)),
            dma((2, 4, 2)),
            dma((2, 4, NX)),
            dma((2, 4, NX)),
            dma((2, 2, NY, 2)),
            dma((2, 2, NY, 2)),
            dma((2, 4, 4)),
            dma((2, 4, 4)),
            dma((2, 2, 2)),
            dma((2, 2, 2)),
        ],
        compiler_params=pltpu.CompilerParams(
            collective_id=0, has_side_effects=True, vmem_limit_bytes=56 * 1024 * 1024
        ),
        cost_estimate=pl.CostEstimate(
            flops=12 * PAD * D * FF, bytes_accessed=10 * 1024 * 1024, transcendentals=2 * PAD * FF
        ),
    )(
        expert_ids.reshape(1, CAP),
        valid_counts,
        gate_values.reshape(1, CAP),
        tokens[0],
        cotangent[0],
        w_in[0],
        w_out.reshape(NY, BLK, D),
    )
    made = pl.pallas_call(
        place,
        out_shape=results,
        in_specs=[hbm] * 4,
        out_specs=(hbm,) * 4,
        scratch_shapes=[pltpu.VMEM(r.shape, r.dtype) for r in results] + [dma((2, 4))],
        compiler_params=pltpu.CompilerParams(vmem_limit_bytes=60 * 1024 * 1024),
    )(*made)
    return tuple(array[None] for array in made)


def solution(mesh):
    placed = (
        P("replica", "expert", None),
        P("replica", "expert", None),
        P("expert", None, None),
        P("expert", None, None),
        P("replica", "expert", None),
        P("replica", "expert", None),
        P("replica", "expert"),
    )
    return jax.shard_map(
        per_device,
        mesh=mesh,
        in_specs=placed,
        out_specs=(
            P("replica", "expert", None),
            P("replica", "expert", None),
            P("expert", "replica", None),
            P("expert", "replica", None),
        ),
        check_vma=False,
    )
```

time: 131 us -> 120 us (0.916)
  the two profiles are of different devices: /device:TPU:16 before, /device:TPU:8 now
where the time goes in v2:
time: 120 us; the launch traced here: 119 us
  Pallas kernels  118 us (98%)
  between operations  1.45 us (1%)
    pallas_call x1, Pallas kernels, per_device(): pl.pallas_call(kernel, out_shape=results, in_specs=[vm] * 3 + [hbm] * 4,...  116 us

profile of v2, /device:TPU:8, one launch (start us, length us, event | category | flops | bytes accessed | tf_op | source)
XLA Modules:
  0.0 119.5 jit_solution(10363983714972067713)
XLA Ops:
  1.3 116.2 %shard_map.102 = (bf16[128,1024]{1,0:T(8,128)(2,1)}, bf16[128,1024]{1,0:T(8,128)(2,1)}, bf16[32,2048]{1,0:T(8,128)(2,1)}, bf16[64,1024]{1,0:T(8,128)(2,1)}) custom-call(s32[1,192]{1,0:T(1,128)} %bitcast.18, s32[1,1]{1,0:T(1,128)S(6)} %copy.11.count, f32[1,192]{1,0:T(1,128)} %bitcast.19, bf16[128,1024]{1,0:T(8,128)(2,1)} %bitcast.12, ...), custom_call_target="tpu_custom_call" | custom-call | flops 6442450944 | bytes 10485760 | tf_op jit(solution)/shard_map/pallas_call | solution.py:495
  117.4 1.9 %shard_map.103 = (bf16[128,1024]{1,0:T(8,128)(2,1)}, bf16[128,1024]{1,0:T(8,128)(2,1)}, bf16[32,2048]{1,0:T(8,128)(2,1)}, bf16[64,1024]{1,0:T(8,128)(2,1)}) custom-call(bf16[128,1024]{1,0:T(8,128)(2,1)} %get-tuple-element.12.refs_0_, bf16[128,1024]{1,0:T(8,128)(2,1)} %get-tuple-element.13.refs_1_, bf16[32,2048]{1,0:T(8,128)(2,1)} %get-tuple-element.14.refs_2_, ...), custom_call_target="tpu_custom_call" | custom-call | tf_op jit(solution)/shard_map/pallas_call | solution.py:560

commit v3 on v2

--- a/solution.py
+++ b/solution.py
@@ -27,6 +27,7 @@
 MESH = pl.DeviceIdType.MESH
 
 ORDER = (4, 3, -3, 2, -2, 1, -1, 0)
+AWAY = ORDER[:-1]
 IDX = {o: i for i, o in enumerate(ORDER)}
 IDX[-4] = 0
 SIGN = (1, -1)
@@ -53,37 +54,39 @@
 
 
 PLAN = (
-    ("toe", 0), ("e", 0, 0, 0), ("e", 1, 0, 1), ("proj",), ("toe", 1), ("toe", 2), ("e", 0, 1, 1),
-    ("e", 1, 1, 0), ("toe", 3), ("toe", 4), ("toe", 5), ("toe", 6), ("e", 0, 1, 0), ("e", 1, 1, 1),
-    ("toe", 7), ("e", 0, 2, 1), ("e", 1, 2, 0), ("e", 0, 2, 0), ("e", 1, 2, 1), ("cb",), ("ti", 0),
-    ("x", 0, 0, (0, 0)), ("x", 1, 0, (0, 1)), ("x", 0, 1, (0, 1)), ("x", 1, 1, (0, 0)), ("tol", 0),
-    ("y", 0, 0, 0), ("y", 0, 0, 1), ("y", 1, 0, 2), ("y", 1, 0, 3), ("ti", 1), ("x", 0, 0, (1, 0)),
-    ("x", 1, 0, (1, 1)), ("x", 0, 1, (1, 1)), ("x", 1, 1, (1, 0)), ("ti", 2), ("x", 0, 0, (2, 0)),
-    ("x", 1, 0, (2, 1)), ("x", 0, 1, (2, 1)), ("x", 1, 1, (2, 0)), ("x", 0, 1, (0, 0)),
-    ("x", 1, 1, (0, 1)), ("tol", 1), ("y", 0, 1, 0), ("y", 0, 1, 2), ("y", 0, 1, 3), ("tol", 2),
-    ("y", 1, 1, 2), ("y", 1, 1, 0), ("y", 1, 1, 1), ("ti", 3), ("y", 0, 1, 1), ("y", 1, 1, 3),
-    ("x", 0, 0, (3, 0)), ("x", 1, 0, (3, 1)), ("x", 0, 1, (1, 0)), ("x", 1, 1, (1, 1)),
-    ("x", 0, 1, (3, 1)), ("x", 1, 1, (3, 0)), ("ti", 4), ("x", 0, 0, (4, 0)), ("x", 1, 0, (4, 1)),
-    ("tol", 3), ("y", 0, 2, 0), ("x", 0, 1, (2, 0)), ("x", 1, 1, (2, 1)), ("y", 0, 2, 2),
-    ("tol", 4), ("y", 1, 2, 0), ("y", 1, 2, 2), ("x", 0, 1, (4, 1)), ("x", 1, 1, (4, 0)), ("ti", 5),
-    ("z1", 0), ("y", 0, 2, 3), ("y", 1, 2, 1), ("x", 0, 0, (5, 0)), ("x", 1, 0, (5, 1)),
-    ("x", 0, 1, (3, 0)), ("y", 0, 2, 1), ("x", 1, 1, (3, 1)), ("y", 1, 2, 3), ("x", 0, 1, (5, 1)),
-    ("x", 1, 1, (5, 0)), ("z1", 1), ("y2", 0, 0, 0), ("tol", 5), ("y2", 1, 1, 0), ("tol", 6),
-    ("ti", 6), ("x", 0, 0, (6, 0)), ("x", 1, 0, (6, 1)), ("x", 0, 1, (6, 1)), ("x", 1, 1, (6, 0)),
-    ("e", 0, 3, 0), ("e", 1, 3, 0), ("x", 0, 1, (4, 0)), ("x", 1, 1, (4, 1)), ("e", 0, 3, 1),
-    ("ti", 7), ("z1", 2), ("x", 0, 0, (7, 0)), ("x", 1, 0, (7, 1)), ("packg",), ("y2", 0, 1, 0),
-    ("x", 0, 1, (5, 0)), ("x", 1, 1, (5, 1)), ("x", 0, 1, (7, 1)), ("x", 1, 1, (7, 0)),
-    ("y2", 1, 2, 0), ("e", 1, 3, 1), ("z1", 3), ("y2", 1, 0, 1), ("y2", 0, 1, 1), ("y", 0, 3, 0),
-    ("y", 0, 3, 1), ("y", 1, 3, 0), ("tol", 7), ("y", 1, 3, 1), ("y", 0, 3, 2), ("y2", 1, 3, 0),
-    ("x", 0, 1, (6, 0)), ("x", 1, 1, (6, 1)), ("y2", 0, 2, 0), ("y2", 0, 2, 1), ("y", 1, 3, 2),
-    ("y", 0, 3, 3), ("y", 1, 3, 3), ("mixed",), ("z1", 4), ("y2", 1, 1, 1), ("ze", 0), ("ze", 1),
-    ("x", 0, 1, (7, 0)), ("x", 1, 1, (7, 1)), ("zl", 0), ("z1", 5), ("y2", 0, 0, 2),
-    ("y2", 1, 1, 2), ("zl", 1), ("y2", 0, 3, 0), ("y2", 0, 3, 1), ("zl", 2), ("z1", 6), ("z1", 7),
-    ("y2", 1, 0, 3), ("y2", 0, 1, 2), ("y2", 0, 1, 3), ("zl", 3), ("x2", 0, 0, 0), ("x2", 1, 0, 1),
-    ("y2", 1, 2, 1), ("x2", 0, 1, 1), ("y2", 1, 2, 2), ("x2", 1, 1, 0), ("fi", 0), ("y2", 1, 1, 3),
-    ("y2", 0, 2, 2), ("y2", 0, 2, 3), ("tgrad",), ("x2", 0, 1, 0), ("y2", 1, 2, 3), ("x2", 1, 1, 1),
-    ("y2", 0, 3, 2), ("y2", 1, 3, 1), ("y2", 0, 3, 3), ("y2", 1, 3, 2), ("y2", 1, 3, 3), ("fo", 0),
-    ("fi", 1), ("fo", 1), ("fi", 2), ("fi", 3),
+    ("toe", 0), ("e", 0, 0, 0), ("e", 1, 0, 1), ("toe", 1), ("toe", 2), ("e", 0, 1, 1),
+    ("e", 1, 1, 0), ("toe", 3), ("toe", 4), ("proj",), ("toe", 5), ("toe", 6), ("toe", 7),
+    ("e", 0, 1, 0), ("e", 1, 1, 1), ("e", 0, 2, 1), ("e", 1, 2, 0), ("e", 0, 2, 0), ("e", 1, 2, 1),
+    ("cb",), ("ti", 0), ("x", 0, 0, (0, 0)), ("x", 1, 0, (0, 1)), ("x", 0, 1, (0, 1)),
+    ("x", 1, 1, (0, 0)), ("tol", 0), ("y", 0, 0, 0), ("y", 1, 0, 2), ("y", 0, 0, 1), ("y", 1, 0, 3),
+    ("ti", 1), ("x", 0, 0, (1, 0)), ("x", 1, 0, (1, 1)), ("x", 0, 1, (1, 1)), ("x", 1, 1, (1, 0)),
+    ("tol", 1), ("y", 0, 1, 2), ("ti", 2), ("x", 0, 0, (2, 0)), ("x", 1, 0, (2, 1)),
+    ("x", 0, 1, (2, 1)), ("x", 1, 1, (2, 0)), ("y", 0, 1, 3), ("tol", 2), ("y", 1, 1, 0),
+    ("x", 0, 1, (0, 0)), ("x", 1, 1, (0, 1)), ("y", 1, 1, 2), ("y", 0, 1, 0), ("y", 1, 1, 1),
+    ("ti", 3), ("x", 0, 0, (3, 0)), ("x", 1, 0, (3, 1)), ("tol", 3), ("y", 0, 1, 1),
+    ("x", 0, 1, (1, 0)), ("x", 1, 1, (1, 1)), ("y", 1, 1, 3), ("ti", 4), ("y", 0, 2, 2),
+    ("x", 0, 0, (4, 0)), ("x", 1, 0, (4, 1)), ("e", 1, 3, 0), ("e", 0, 3, 0), ("e", 1, 3, 1),
+    ("x", 0, 1, (2, 0)), ("x", 1, 1, (2, 1)), ("tol", 4), ("y", 0, 2, 3), ("x", 0, 1, (3, 1)),
+    ("x", 1, 1, (3, 0)), ("y", 1, 2, 0), ("ti", 5), ("z1", 0), ("y", 0, 2, 0), ("x", 0, 0, (5, 0)),
+    ("x", 1, 0, (5, 1)), ("y", 1, 2, 1), ("ti", 6), ("x", 0, 0, (6, 0)), ("x", 1, 0, (6, 1)),
+    ("tol", 5), ("y", 0, 2, 1), ("y", 1, 2, 2), ("z1", 1), ("x", 0, 1, (3, 0)), ("x", 1, 1, (3, 1)),
+    ("tol", 6), ("y", 0, 3, 2), ("y", 1, 2, 3), ("x", 0, 1, (4, 0)), ("x", 1, 1, (4, 1)), ("ti", 7),
+    ("z1", 2), ("packg",), ("x", 0, 1, (5, 0)), ("x", 1, 1, (5, 1)), ("x", 0, 1, (4, 1)),
+    ("x", 1, 1, (4, 0)), ("y", 0, 3, 0), ("x", 0, 1, (5, 1)), ("y", 1, 3, 0), ("x", 1, 1, (5, 0)),
+    ("y", 0, 3, 3), ("y", 1, 3, 1), ("x", 0, 1, (6, 0)), ("x", 1, 1, (6, 1)), ("z1", 3),
+    ("y", 0, 3, 1), ("y", 1, 3, 2), ("x", 0, 1, (6, 1)), ("x", 1, 1, (6, 0)), ("y2", 0, 0, 0),
+    ("y2", 1, 0, 1), ("y", 1, 3, 3), ("y2", 0, 1, 1), ("e", 0, 3, 1), ("x", 0, 0, (7, 0)),
+    ("x", 1, 0, (7, 1)), ("ze", 0), ("mixed",), ("x", 0, 1, (7, 1)), ("x", 1, 1, (7, 0)),
+    ("y2", 1, 1, 0), ("tol", 7), ("z1", 4), ("zl", 0), ("z1", 5), ("y2", 0, 0, 2), ("y2", 1, 1, 2),
+    ("zl", 1), ("zl", 2), ("y2", 0, 1, 0), ("y2", 1, 1, 1), ("y2", 0, 2, 1), ("z1", 6),
+    ("y2", 1, 0, 3), ("y2", 0, 1, 3), ("zl", 3), ("x", 0, 1, (7, 0)), ("x", 1, 1, (7, 1)),
+    ("y2", 1, 2, 0), ("y2", 0, 1, 2), ("y2", 1, 2, 2), ("ze", 1), ("x2", 0, 0, 0), ("x2", 1, 0, 1),
+    ("y2", 1, 1, 3), ("y2", 0, 2, 0), ("y2", 1, 2, 1), ("y2", 0, 2, 3), ("x2", 0, 1, 1),
+    ("x2", 1, 1, 0), ("y2", 0, 3, 1), ("y2", 1, 3, 0), ("y2", 0, 2, 2), ("z1", 7), ("dd", -3),
+    ("dd", 3), ("dd", -2), ("y2", 1, 2, 3), ("dd", 2), ("dd", 4), ("dd", 1), ("x2", 0, 1, 0),
+    ("x2", 1, 1, 1), ("tgrad",), ("dd", -1), ("y2", 0, 3, 0), ("y2", 1, 3, 1), ("y2", 0, 3, 2),
+    ("y2", 1, 3, 2), ("y2", 0, 3, 3), ("y2", 1, 3, 3), ("fo", 0), ("fo", 1), ("fd",), ("fi", 0),
+    ("fi", 1), ("fi", 2), ("fi", 3),
 )
 
 
@@ -132,13 +135,47 @@
             out.wait_send()
 
 
+class Spread:
+    def __init__(self, own, buf, ssem, rsem, peer):
+        self.own, self.buf, self.ssem, self.rsem, self.peer = own, buf, ssem, rsem, peer
+        self.sent = []
+
+    def copy(self, o, src):
+        k = AWAY.index(o)
+        return pltpu.make_async_remote_copy(
+            src_ref=src,
+            dst_ref=self.buf.at[k],
+            send_sem=self.ssem.at[k],
+            recv_sem=self.rsem.at[k],
+            device_id=self.peer(o),
+            device_id_type=MESH,
+        )
+
+    def send(self, o):
+        out = self.copy(o, self.own(o))
+        out.start()
+        self.sent.append(out)
+
+    def last(self):
+        total = self.own(0)[...].astype(F32)
+        for k, o in enumerate(AWAY):
+            self.copy(o, self.buf.at[k]).wait_recv()
+            total = total + self.buf[k].astype(F32)
+        return total
+
+    def drain(self):
+        for out in self.sent:
+            out.wait_send()
+
+
 def kernel(
-    ids_r, count, gate_r, tok_hbm, cot_hbm, w_in_hbm, w_out_hbm,
-    mixed, tgrad, gwin, gwout,
+    ids_hbm, count_hbm, gate_hbm, tok_hbm, cot_hbm, w_in_hbm, w_out_hbm,
+    mixed_hbm, tgrad_hbm, gwin_hbm, gwout_hbm,
+    ids_r, count, gate_r, mixed, tgrad, gwin, gwout,
     tok, cot, wi, wo, code_s, code_r, out_s, out_r, back_s, back_r, at,
     xs, xt, us, hid, hid_t, slopes, proj, ig, ti, toe, tol, z1, z2,
-    yer, yr, xr, y2r, x2r,
-    lsem, csem, asem, bsem, yes, yev, ys, yv, xsd, xv, y2s, y2v, x2s, x2v,
+    yer, yr, xr, y2r, x2r, ddr,
+    lsem, osem, csem, asem, bsem, yes, yev, ys, yv, xsd, xv, y2s, y2v, x2s, x2v, dds, ddv,
 ):
     rep = lax.axis_index("replica")
     me = lax.axis_index("expert")
@@ -155,17 +192,27 @@
             barrier, inc=1, device_id={"expert": (me + k) % NE}, device_id_type=MESH
         )
 
-    for peer in y_peers + x_peers:
+    for g in range(1, NY):
+        peer = {"replica": ((py + g) % NY) * NX + px}
+        pl.semaphore_signal(barrier, inc=1, device_id=peer, device_id_type=MESH)
+    for peer in x_peers:
         pl.semaphore_signal(barrier, inc=1, device_id=peer, device_id_type=MESH)
 
     loads = [
         pltpu.make_async_copy(here, there, lsem.at[n])
         for n, (here, there) in enumerate(
-            ((tok_hbm, tok), (cot_hbm, cot), (w_in_hbm, wi), (w_out_hbm, wo))
+            (
+                (tok_hbm, tok), (cot_hbm, cot), (w_in_hbm, wi), (w_out_hbm, wo),
+                (ids_hbm, ids_r), (count_hbm, count), (gate_hbm, gate_r),
+            )
         )
     ]
+    loads = loads[4:] + loads[:4]
     for load in loads:
         load.start()
+    for load in loads[:3]:
+        load.wait()
+    loads = loads[3:]
 
     n_live = count[...]
     row_ids = ids_r[...]
@@ -181,7 +228,7 @@
     code = present * (nn(present.astype(BF), before_me) + 1.0)
     code_s[...] = jnp.broadcast_to(code[:, None, :], (NE, 16, TOK)).astype(BF)
 
-    pl.semaphore_wait(barrier, NE - 1 + 4)
+    pl.semaphore_wait(barrier, NE - 1 + NY - 1 + 2)
 
     def scatter(src, dst, ssem, rsem, part=None):
         def cut(ref, e):
@@ -322,12 +369,19 @@
     )
     flow_y2 = Ring(
         NY,
-        lambda o, p: z1.at[(py + (o + NY)) % NY, pl.ds(2 * p, 2)],
-        lambda d, s, p: y2r.at[d, s, p],
+        lambda o, p: z1.at[(py + (o + NY)) % NY, pl.ds(2 * p, 2 - p // 3)],
+        lambda d, s, p: y2r.at[d, s, p, pl.ds(0, 2 - p // 3)],
         lambda d, s, p: y2s.at[d, s, p],
         lambda d, s, p: y2v.at[d, s, p],
         y_peers,
         lambda p: p % 2,
+    )
+    flow_d = Spread(
+        lambda o: z1.at[(py + (o + NY)) % NY, NY - 1],
+        ddr,
+        dds,
+        ddv,
+        lambda o: {"replica": ((py + (o + NY)) % NY) * NX + px},
     )
     flow_x2 = Ring(
         NX,
@@ -411,6 +465,13 @@
     def late_z2(c):
         z2[c, :, :, EARLY:] = flow_y.last(c).astype(BF).reshape(2, 32, D - EARLY)
 
+    stores = [
+        pltpu.make_async_copy(here, there, osem.at[n])
+        for n, (here, there) in enumerate(
+            ((mixed, mixed_hbm), (tgrad, tgrad_hbm), (gwin, gwin_hbm), (gwout, gwout_hbm))
+        )
+    ]
+
     def gather(a, dest):
         whole(back_r.at[a], bsem.at[1, a])
         sums = [None] * NC
@@ -421,14 +482,18 @@
                 sums[c] = part if sums[c] is None else sums[c] + part
         for c in range(NC):
             dest[:, c * 128 : (c + 1) * 128] = sums[c].astype(BF)
+        stores[a].start()
 
     scale = 1.0 / (NX * NY)
 
     def finish_in(p):
         total = (flow_y2.last(p) * scale).astype(BF)
-        for k in range(2):
+        for k in range(2 - p // 3):
             at_b = (2 * p + k) * BLK
             gwin[:, at_b : at_b + BLK] = total[k]
+
+    def finish_direct():
+        gwin[:, FF - BLK :] = (flow_d.last() * scale).astype(BF)
 
     def finish_out(p):
         gwout[p * 32 : (p + 1) * 32] = (flow_x2.last(p) * scale).astype(BF)
@@ -452,13 +517,17 @@
         "tgrad": lambda: gather(1, tgrad),
         "fi": finish_in,
         "fo": finish_out,
+        "dd": flow_d.send,
+        "fd": finish_direct,
     }
     whole(out_r.at[1], asem.at[1, 1], first)
     unpack(1, range(EARLY // 128), put_u)
     for name, *at_step in PLAN:
         steps[name](*at_step)
 
-    for flow in (flow_e, flow_y, flow_x, flow_y2, flow_x2):
+    stores[2].start()
+    stores[3].start()
+    for flow in (flow_e, flow_y, flow_x, flow_y2, flow_x2, flow_d):
         flow.drain()
     whole(code_s, csem.at[0])
     whole(out_s.at[0], asem.at[0, 0])
@@ -466,6 +535,8 @@
     whole(out_s.at[1], asem.at[0, 2], second)
     for a in (0, 1):
         whole(back_s.at[a], bsem.at[0, a])
+    for store in stores:
+        store.wait()
 
 
 def place(*refs):
@@ -481,7 +552,6 @@
 
 
 def per_device(tokens, cotangent, w_in, w_out, gate_values, expert_ids, valid_counts):
-    vm = pl.BlockSpec(memory_space=pltpu.VMEM)
     hbm = pl.BlockSpec(memory_space=pl.ANY)
     dma = pltpu.SemaphoreType.DMA
     blocks = (2, NE, NQ, 16, 128)
@@ -495,9 +565,15 @@
     made = pl.pallas_call(
         kernel,
         out_shape=results,
-        in_specs=[vm] * 3 + [hbm] * 4,
-        out_specs=(vm,) * 4,
+        in_specs=[hbm] * 7,
+        out_specs=(hbm,) * 4,
         scratch_shapes=[
+            pltpu.VMEM((1, CAP), I32),
+            pltpu.VMEM((1, 1), I32),
+            pltpu.VMEM((1, CAP), F32),
+        ]
+        + [pltpu.VMEM(r.shape, r.dtype) for r in results]
+        + [
             pltpu.VMEM((TOK, D), BF),
             pltpu.VMEM((TOK, D), BF),
             pltpu.VMEM((D, FF), BF),
@@ -527,6 +603,8 @@
             pltpu.VMEM((2, 2, NY, 2, NY // 2, 32, BLK), BF),
             pltpu.VMEM((2, 4, 4, 2, 32, BLK), BF),
             pltpu.VMEM((2, 2, 2, 32, D), BF),
+            pltpu.VMEM((NY - 1, 32, BLK), BF),
+            dma((7,)),
             dma((4,)),
             dma((2,)),
             dma((2, 3)),
@@ -541,6 +619,8 @@
             dma((2, 4, 4)),
             dma((2, 2, 2)),
             dma((2, 2, 2)),
+            dma((NY - 1,)),
+            dma((NY - 1,)),
         ],
         compiler_params=pltpu.CompilerParams(
             collective_id=0, has_side_effects=True, vmem_limit_bytes=56 * 1024 * 1024

time: 120 us -> 115 us (0.958)
  the two profiles are of different devices: /device:TPU:8 before, /device:TPU:16 now
where the time goes in v3:
time: 115 us
  Pallas kernels  114 us (99%)
  between operations  1.45 us (1%)
    pallas_call x1, Pallas kernels, per_device(): pl.pallas_call(kernel, out_shape=results, in_specs=[hbm] * 7, out_specs=(...  112 us

profile of v3, /device:TPU:16, one launch (start us, length us, event | category | flops | bytes accessed | tf_op | source)
XLA Modules:
  0.0 115.1 jit_solution(16326535739671144145)
XLA Ops:
  1.3 111.7 %shard_map.102 = (bf16[128,1024]{1,0:T(8,128)(2,1)}, bf16[128,1024]{1,0:T(8,128)(2,1)}, bf16[32,2048]{1,0:T(8,128)(2,1)}, bf16[64,1024]{1,0:T(8,128)(2,1)}) custom-call(s32[1,192]{1,0:T(1,128)} %bitcast.18, s32[1,1]{1,0:T(1,128)S(6)} %copy.11.count_hbm, f32[1,192]{1,0:T(1,128)} %bitcast.19, bf16[128,1024]{1,0:T(8,128)(2,1)} %bitcast.12, ...), custom_call_target="tpu_custom_call" | custom-call | flops 6442450944 | bytes 10485760 | tf_op jit(solution)/shard_map/pallas_call | solution.py:565
  113.0 1.9 %shard_map.103 = (bf16[128,1024]{1,0:T(8,128)(2,1)}, bf16[128,1024]{1,0:T(8,128)(2,1)}, bf16[32,2048]{1,0:T(8,128)(2,1)}, bf16[64,1024]{1,0:T(8,128)(2,1)}) custom-call(bf16[128,1024]{1,0:T(8,128)(2,1)} %get-tuple-element.12.refs_0_, bf16[128,1024]{1,0:T(8,128)(2,1)} %get-tuple-element.13.refs_1_, bf16[32,2048]{1,0:T(8,128)(2,1)} %get-tuple-element.14.refs_2_, ...), custom_call_target="tpu_custom_call" | custom-call | tf_op jit(solution)/shard_map/pallas_call | solution.py:640
